TPU v7x, 512 devices: a whole 4x8x8 slice. The times are simulated.
512 devices in a mesh: seq: 32 (over y_lo, z, core), grp: 16 (over y_hi, x).
Axes of the slice: x: 4, y: 8 (y_hi: 4, y_lo: 2; y = y_hi * 2 + y_lo), z: 8, core: 2. Of those that a mesh axis runs over, the one named last changes fastest.
Arguments:
- text_q: bfloat16 [16, 8192, 1024], P('grp', 'seq'), may hold values from -6 to 6
- cross_q: bfloat16 [16, 8192, 1024], P('grp', 'seq'), may hold values from -6 to 6
- text_k: bfloat16 [16, 8192, 128], P('grp', 'seq'), may hold values from -6 to 6
- text_v: bfloat16 [16, 8192, 128], P('grp', 'seq'), may hold values from -12 to 12
- frame_k: bfloat16 [16, 512, 128], P('grp', 'seq'), may hold values from -6 to 6
- frame_v: bfloat16 [16, 512, 128], P('grp', 'seq'), may hold values from -12 to 12
- block_pos: int32 [32], replicated, may hold values from 0 to 31, each once
- frame_mask: int32 [32, 16], replicated, may hold values from 0 to 1, as said below
Outputs:
- self_out: bfloat16 [16, 8192, 1024], P('grp', 'seq')
- cross_out: bfloat16 [16, 8192, 1024], P('grp', 'seq')
Inputs may be any that keep to these rules, and one draw needn't show every extreme that they name: `frame_mask`: every row has at least one 1.
All inputs are finite; a program needn't handle non-finite values.
Results may differ from a plain program's by a relative error of at most 0.008.
Values may be sent and summed in bfloat16 or wider, within the bound.
No kernel may reach another device: no remote copies, remote signals or barrier semaphores. Data moves between devices by JAX's collectives and lax.ppermute only.
A program may use at most 64 MiB of HBM per device.

v0:
```python
import jax
import jax.numpy as jnp
from jax import lax
from jax.sharding import PartitionSpec as P

H = 8


def shifted(value, axis, steps):
    count = lax.axis_size(axis)
    pairs = [(source, (source + steps) % count) for source in range(count)]
    return lax.ppermute(value, axis, pairs)


def attend_tile(running, queries, key_rows, value_rows, allowed, factor):
    row_max, row_sum, weighted = running
    scores = (
        jnp.einsum("thd,kd->thk", queries, key_rows, preferred_element_type=jnp.float32) * factor
    )
    if allowed is not None:
        scores = jnp.where(allowed[:, None, :], scores, jnp.float32(-1e30))
    new_max = jnp.maximum(row_max, jnp.max(scores, axis=-1))
    shrink = jnp.exp(row_max - new_max)
    weights = jnp.exp(scores - new_max[..., None])
    if allowed is not None:
        weights = jnp.where(allowed[:, None, :], weights, jnp.float32(0.0))
    new_sum = row_sum * shrink + jnp.sum(weights, axis=-1)
    product = jnp.einsum(
        "thk,kd->thd", weights.astype(jnp.bfloat16), value_rows, preferred_element_type=jnp.float32
    )
    return (new_max, new_sum, weighted * shrink[..., None] + product)


def empty_state(tok_rows, head_dim):
    return (
        jnp.full((tok_rows, H), -1e30, jnp.float32),
        jnp.zeros((tok_rows, H), jnp.float32),
        jnp.zeros((tok_rows, H, head_dim), jnp.float32),
    )


def finish(running, tok_rows):
    row_max, row_sum, weighted = running
    result = weighted / row_sum[..., None]
    return result.reshape(1, tok_rows, -1).astype(jnp.bfloat16)


def per_device(text_q, cross_q, text_k, text_v, frame_k, frame_v, block_pos, frame_mask):
    tok_rows = text_q.shape[1]
    head_dim = text_k.shape[-1]
    factor = head_dim ** (-0.5)
    seq_count = lax.axis_size("seq")
    my_index = lax.axis_index("seq")
    my_block = block_pos[my_index]
    row_ids = jnp.arange(tok_rows, dtype=jnp.int32)
    query_pos = my_block * tok_rows + row_ids
    queries = text_q[0].reshape(tok_rows, H, head_dim)
    cross_rows = cross_q[0].reshape(tok_rows, H, head_dim)

    def self_tile(running, stacked, source, active):
        source_block = block_pos[source]
        causal = (source_block * tok_rows + row_ids)[None, :] <= query_pos[:, None]

        def self_compute(state):
            return attend_tile(state, queries, stacked[0], stacked[1], causal, factor)

        def self_keep(state):
            return state

        return lax.cond(
            jnp.logical_and(active, source_block <= my_block), self_compute, self_keep, running
        )

    stacked_own = jnp.stack([text_k[0], text_v[0]])
    running = self_tile(empty_state(tok_rows, head_dim), stacked_own, my_index, jnp.bool_(True))

    def one_hop(hops, state):
        current, stacked = state
        stacked = shifted(stacked, "seq", 1)
        source = (my_index - hops) % seq_count
        return (self_tile(current, stacked, source, jnp.bool_(True)), stacked)

    running, _ = lax.fori_loop(1, seq_count, one_hop, (running, stacked_own))
    self_out = finish(running, tok_rows)
    mask_row = frame_mask[my_block]

    def frame_tile(state, frame_id, key_rows, value_rows):

        def frame_compute(inner):
            return attend_tile(inner, cross_rows, key_rows, value_rows, None, factor)

        def frame_keep(inner):
            return inner

        return lax.cond(mask_row[frame_id] > 0, frame_compute, frame_keep, state)

    whole_frames = (
        lax.all_gather(frame_k, "seq", axis=1, tiled=True),
        lax.all_gather(frame_v, "seq", axis=1, tiled=True),
    )
    piece_k = lax.all_gather(whole_frames[0], "grp", axis=0, tiled=True)
    piece_v = lax.all_gather(whole_frames[1], "grp", axis=0, tiled=True)

    def one_frame(frame_slot, inner):
        key_rows = lax.dynamic_index_in_dim(piece_k, frame_slot, 0, keepdims=False)
        value_rows = lax.dynamic_index_in_dim(piece_v, frame_slot, 0, keepdims=False)
        return frame_tile(inner, frame_slot, key_rows, value_rows)

    crossed = lax.fori_loop(0, piece_k.shape[0], one_frame, empty_state(tok_rows, head_dim))
    cross_out = finish(crossed, tok_rows)
    return (self_out, cross_out)


def solution(mesh):
    return jax.shard_map(
        per_device,
        mesh=mesh,
        in_specs=(
            P("grp", "seq", None),
            P("grp", "seq", None),
            P("grp", "seq", None),
            P("grp", "seq", None),
            P("grp", "seq", None),
            P("grp", "seq", None),
            P(),
            P(),
        ),
        out_specs=(P("grp", "seq", None), P("grp", "seq", None)),
        check_vma=False,
    )
```

profile of v0, /device:TPU:18, one launch (start us, length us, event | category | flops | bytes accessed | tf_op | source)
XLA Modules:
  0.0 504.2 jit_solution(4209707876359475496)
XLA Ops:
  7.2 43.8 %all_gather.12 = bf16[1,512,128]{2,1,0:T(8,128)(2,1)} all-gather(bf16[1,16,128]{2,1,0:T(8,128)(2,1)} %param.20), channel_id=1, replica_groups=mesh['seq'=32,'grp'=16] {'seq'}, dimensions={1}, use_global_device_ids=true | all-gather | bytes 135168 | tf_op jit(solution)/shard_map/all_gather | solution.py:98
  51.1 34.0 %all_gather.14 = bf16[1,512,128]{2,1,0:T(8,128)(2,1)} all-gather(bf16[1,16,128]{2,1,0:T(8,128)(2,1)} %param.21), channel_id=1, replica_groups=mesh['seq'=32,'grp'=16] {'seq'}, dimensions={1}, use_global_device_ids=true | all-gather | bytes 135168 | tf_op jit(solution)/shard_map/all_gather | solution.py:99
  92.8 344.1 %while.40 = (s32[]{:T(128)}, f32[256,8]{0,1:T(8,128)S(1)}, f32[256,8]{0,1:T(8,128)S(1)}, f32[256,8,128]{2,0,1:T(8,128)S(1)}, bf16[2,256,128]{2,1,0:T(8,128)(2,1)...) while((s32[]{:T(128)}, f32[256,8]{0,1:T(8,128)S(1)}, ...), condition=%wide.region_7.8_spmd.clone, body=%wide.region_2.7_spmd.clone.sunk | while | flops 275845664 | bytes 10231286 | solution.py:83
  97.2 10.5 %collective-permute-done = bf16[2,256,128]{2,1,0:T(8,128)(2,1)S(1)} collective-permute-done((bf16[2,256,128]{2,1,0:T(8,128)(2,1)S(1)}, bf16[2,256,128]{2,1,0:T(8,128)(2,1)S(1)}, u32[]{:S(2)}, u32[]{:S(2)}) %collective-permute-start) | collective-permute-done | bytes 131104 | tf_op jit(solution)/shard_map/while/body/eval_jaxpr/ppermute | solution.py:12
  111.6 4.5 collective-permute-done
  122.9 4.5 collective-permute-done
  134.2 5.8 %collective-permute-done = bf16[2,256,128]{2,1,0:T(8,128)(2,1)S(1)} collective-permute-done((bf16[2,256,128]{2,1,0:T(8,128)(2,1)S(1)}, bf16[2,256,128]{2,1,0:T(8,128)(2,1)S(1)}, u32[]{:S(2)}, u32[]{:S(2)}) %collective-permute-start) | collective-permute-done | bytes 131104 | tf_op jit(solution)/shard_map/while/body/eval_jaxpr/ppermute | solution.py:12
  143.9 4.5 collective-permute-done
  155.2 5.6 %collective-permute-done = bf16[2,256,128]{2,1,0:T(8,128)(2,1)S(1)} collective-permute-done((bf16[2,256,128]{2,1,0:T(8,128)(2,1)S(1)}, bf16[2,256,128]{2,1,0:T(8,128)(2,1)S(1)}, u32[]{:S(2)}, u32[]{:S(2)}) %collective-permute-start) | collective-permute-done | bytes 131104 | tf_op jit(solution)/shard_map/while/body/eval_jaxpr/ppermute | solution.py:12
  167.5 10.2 %collective-permute-done = bf16[2,256,128]{2,1,0:T(8,128)(2,1)S(1)} collective-permute-done((bf16[2,256,128]{2,1,0:T(8,128)(2,1)S(1)}, bf16[2,256,128]{2,1,0:T(8,128)(2,1)S(1)}, u32[]{:S(2)}, u32[]{:S(2)}) %collective-permute-start) | collective-permute-done | bytes 131104 | tf_op jit(solution)/shard_map/while/body/eval_jaxpr/ppermute | solution.py:12
  184.4 4.5 collective-permute-done
  195.7 4.5 collective-permute-done
  207.0 4.5 collective-permute-done
  215.4 4.5 collective-permute-done
  226.7 4.5 collective-permute-done
  238.0 4.5 collective-permute-done
  249.2 4.5 collective-permute-done
  257.7 4.5 collective-permute-done
  268.9 4.5 collective-permute-done
  280.2 4.5 collective-permute-done
  291.5 4.5 collective-permute-done
  302.8 4.5 collective-permute-done
  314.0 4.5 collective-permute-done
  325.3 4.5 collective-permute-done
  333.7 4.5 collective-permute-done
  345.0 4.5 collective-permute-done
  356.3 4.5 collective-permute-done
  367.6 4.5 collective-permute-done
  378.8 4.5 collective-permute-done
  407.0 4.5 collective-permute-done
  418.3 4.5 collective-permute-done
  439.7 56.0 %while.39 = (s32[]{:T(128)}, f32[256,8]{0,1:T(8,128)S(1)}, f32[256,8]{0,1:T(8,128)S(1)}, f32[256,8,128]{2,0,1:T(8,128)S(1)}, s32[16]{0:T(128)S(1)}, /*index=5*/b...) while((s32[]{:T(128)}, f32[256,8]{0,1:T(8,128)S(1)}, ...), condition=%wide.region_13.14_spmd, body=%wide.region_8.13_spmd.sunk | while | flops 545787904 | bytes 15598831 | solution.py:109
  (469 shorter events, 302.5 us)
Async XLA Ops:
  7.2 432.4 %all-gather.3.cloned.1.call-start = ((), (), s32[]{:S(2)}) async-start(), calls=%async_computation | async-start | bytes 2228224 | tf_op jit(solution)/shard_map/all_gather | solution.py:101
  51.1 388.5 %all-gather.5.cloned.1.call-start = ((), (), s32[]{:S(2)}) async-start(), calls=%async_computation.1 | async-start | bytes 2228224 | tf_op jit(solution)/shard_map/all_gather | solution.py:102
  92.8 14.9 %collective-permute-start = (bf16[2,256,128]{2,1,0:T(8,128)(2,1)S(1)}, bf16[2,256,128]{2,1,0:T(8,128)(2,1)S(1)}, u32[]{:S(2)}, u32[]{:S(2)}) collective-permute-start(bf16[2,256,128]{2,1,0:T(8,128)(2,1)S(1)} %get-tuple-element.836), channel_id=1, source_target_pairs={{0,16},{16,32},{32,48},{48,64},{64,80},{80,96},{96,112},{112,128},... | collective-permute-start | bytes 393224 | tf_op jit(solution)/shard_map/while/body/eval_jaxpr/ppermute | solution.py:12
  107.7 8.4 %collective-permute-start = (bf16[2,256,128]{2,1,0:T(8,128)(2,1)S(1)}, bf16[2,256,128]{2,1,0:T(8,128)(2,1)S(1)}, u32[]{:S(2)}, u32[]{:S(2)}) collective-permute-start(bf16[2,256,128]{2,1,0:T(8,128)(2,1)S(1)} %get-tuple-element.836), channel_id=1, source_target_pairs={{0,16},{16,32},{32,48},{48,64},{64,80},{80,96},{96,112},{112,128},... | collective-permute-start | bytes 393224 | tf_op jit(solution)/shard_map/while/body/eval_jaxpr/ppermute | solution.py:12
  119.0 8.4 %collective-permute-start = (bf16[2,256,128]{2,1,0:T(8,128)(2,1)S(1)}, bf16[2,256,128]{2,1,0:T(8,128)(2,1)S(1)}, u32[]{:S(2)}, u32[]{:S(2)}) collective-permute-start(bf16[2,256,128]{2,1,0:T(8,128)(2,1)S(1)} %get-tuple-element.836), channel_id=1, source_target_pairs={{0,16},{16,32},{32,48},{48,64},{64,80},{80,96},{96,112},{112,128},... | collective-permute-start | bytes 393224 | tf_op jit(solution)/shard_map/while/body/eval_jaxpr/ppermute | solution.py:12
  130.3 9.7 %collective-permute-start = (bf16[2,256,128]{2,1,0:T(8,128)(2,1)S(1)}, bf16[2,256,128]{2,1,0:T(8,128)(2,1)S(1)}, u32[]{:S(2)}, u32[]{:S(2)}) collective-permute-start(bf16[2,256,128]{2,1,0:T(8,128)(2,1)S(1)} %get-tuple-element.836), channel_id=1, source_target_pairs={{0,16},{16,32},{32,48},{48,64},{64,80},{80,96},{96,112},{112,128},... | collective-permute-start | bytes 393224 | tf_op jit(solution)/shard_map/while/body/eval_jaxpr/ppermute | solution.py:12
  140.0 8.4 %collective-permute-start = (bf16[2,256,128]{2,1,0:T(8,128)(2,1)S(1)}, bf16[2,256,128]{2,1,0:T(8,128)(2,1)S(1)}, u32[]{:S(2)}, u32[]{:S(2)}) collective-permute-start(bf16[2,256,128]{2,1,0:T(8,128)(2,1)S(1)} %get-tuple-element.836), channel_id=1, source_target_pairs={{0,16},{16,32},{32,48},{48,64},{64,80},{80,96},{96,112},{112,128},... | collective-permute-start | bytes 393224 | tf_op jit(solution)/shard_map/while/body/eval_jaxpr/ppermute | solution.py:12
  151.3 9.4 %collective-permute-start = (bf16[2,256,128]{2,1,0:T(8,128)(2,1)S(1)}, bf16[2,256,128]{2,1,0:T(8,128)(2,1)S(1)}, u32[]{:S(2)}, u32[]{:S(2)}) collective-permute-start(bf16[2,256,128]{2,1,0:T(8,128)(2,1)S(1)} %get-tuple-element.836), channel_id=1, source_target_pairs={{0,16},{16,32},{32,48},{48,64},{64,80},{80,96},{96,112},{112,128},... | collective-permute-start | bytes 393224 | tf_op jit(solution)/shard_map/while/body/eval_jaxpr/ppermute | solution.py:12
  163.6 14.0 %collective-permute-start = (bf16[2,256,128]{2,1,0:T(8,128)(2,1)S(1)}, bf16[2,256,128]{2,1,0:T(8,128)(2,1)S(1)}, u32[]{:S(2)}, u32[]{:S(2)}) collective-permute-start(bf16[2,256,128]{2,1,0:T(8,128)(2,1)S(1)} %get-tuple-element.836), channel_id=1, source_target_pairs={{0,16},{16,32},{32,48},{48,64},{64,80},{80,96},{96,112},{112,128},... | collective-permute-start | bytes 393224 | tf_op jit(solution)/shard_map/while/body/eval_jaxpr/ppermute | solution.py:12
  180.5 8.4 %collective-permute-start = (bf16[2,256,128]{2,1,0:T(8,128)(2,1)S(1)}, bf16[2,256,128]{2,1,0:T(8,128)(2,1)S(1)}, u32[]{:S(2)}, u32[]{:S(2)}) collective-permute-start(bf16[2,256,128]{2,1,0:T(8,128)(2,1)S(1)} %get-tuple-element.836), channel_id=1, source_target_pairs={{0,16},{16,32},{32,48},{48,64},{64,80},{80,96},{96,112},{112,128},... | collective-permute-start | bytes 393224 | tf_op jit(solution)/shard_map/while/body/eval_jaxpr/ppermute | solution.py:12
  191.8 8.4 %collective-permute-start = (bf16[2,256,128]{2,1,0:T(8,128)(2,1)S(1)}, bf16[2,256,128]{2,1,0:T(8,128)(2,1)S(1)}, u32[]{:S(2)}, u32[]{:S(2)}) collective-permute-start(bf16[2,256,128]{2,1,0:T(8,128)(2,1)S(1)} %get-tuple-element.836), channel_id=1, source_target_pairs={{0,16},{16,32},{32,48},{48,64},{64,80},{80,96},{96,112},{112,128},... | collective-permute-start | bytes 393224 | tf_op jit(solution)/shard_map/while/body/eval_jaxpr/ppermute | solution.py:12
  203.1 8.4 %collective-permute-start = (bf16[2,256,128]{2,1,0:T(8,128)(2,1)S(1)}, bf16[2,256,128]{2,1,0:T(8,128)(2,1)S(1)}, u32[]{:S(2)}, u32[]{:S(2)}) collective-permute-start(bf16[2,256,128]{2,1,0:T(8,128)(2,1)S(1)} %get-tuple-element.836), channel_id=1, source_target_pairs={{0,16},{16,32},{32,48},{48,64},{64,80},{80,96},{96,112},{112,128},... | collective-permute-start | bytes 393224 | tf_op jit(solution)/shard_map/while/body/eval_jaxpr/ppermute | solution.py:12
  211.5 8.4 %collective-permute-start = (bf16[2,256,128]{2,1,0:T(8,128)(2,1)S(1)}, bf16[2,256,128]{2,1,0:T(8,128)(2,1)S(1)}, u32[]{:S(2)}, u32[]{:S(2)}) collective-permute-start(bf16[2,256,128]{2,1,0:T(8,128)(2,1)S(1)} %get-tuple-element.836), channel_id=1, source_target_pairs={{0,16},{16,32},{32,48},{48,64},{64,80},{80,96},{96,112},{112,128},... | collective-permute-start | bytes 393224 | tf_op jit(solution)/shard_map/while/body/eval_jaxpr/ppermute | solution.py:12
  222.8 8.4 %collective-permute-start = (bf16[2,256,128]{2,1,0:T(8,128)(2,1)S(1)}, bf16[2,256,128]{2,1,0:T(8,128)(2,1)S(1)}, u32[]{:S(2)}, u32[]{:S(2)}) collective-permute-start(bf16[2,256,128]{2,1,0:T(8,128)(2,1)S(1)} %get-tuple-element.836), channel_id=1, source_target_pairs={{0,16},{16,32},{32,48},{48,64},{64,80},{80,96},{96,112},{112,128},... | collective-permute-start | bytes 393224 | tf_op jit(solution)/shard_map/while/body/eval_jaxpr/ppermute | solution.py:12
  234.1 8.4 %collective-permute-start = (bf16[2,256,128]{2,1,0:T(8,128)(2,1)S(1)}, bf16[2,256,128]{2,1,0:T(8,128)(2,1)S(1)}, u32[]{:S(2)}, u32[]{:S(2)}) collective-permute-start(bf16[2,256,128]{2,1,0:T(8,128)(2,1)S(1)} %get-tuple-element.836), channel_id=1, source_target_pairs={{0,16},{16,32},{32,48},{48,64},{64,80},{80,96},{96,112},{112,128},... | collective-permute-start | bytes 393224 | tf_op jit(solution)/shard_map/while/body/eval_jaxpr/ppermute | solution.py:12
  245.4 8.4 %collective-permute-start = (bf16[2,256,128]{2,1,0:T(8,128)(2,1)S(1)}, bf16[2,256,128]{2,1,0:T(8,128)(2,1)S(1)}, u32[]{:S(2)}, u32[]{:S(2)}) collective-permute-start(bf16[2,256,128]{2,1,0:T(8,128)(2,1)S(1)} %get-tuple-element.836), channel_id=1, source_target_pairs={{0,16},{16,32},{32,48},{48,64},{64,80},{80,96},{96,112},{112,128},... | collective-permute-start | bytes 393224 | tf_op jit(solution)/shard_map/while/body/eval_jaxpr/ppermute | solution.py:12
  253.8 8.4 %collective-permute-start = (bf16[2,256,128]{2,1,0:T(8,128)(2,1)S(1)}, bf16[2,256,128]{2,1,0:T(8,128)(2,1)S(1)}, u32[]{:S(2)}, u32[]{:S(2)}) collective-permute-start(bf16[2,256,128]{2,1,0:T(8,128)(2,1)S(1)} %get-tuple-element.836), channel_id=1, source_target_pairs={{0,16},{16,32},{32,48},{48,64},{64,80},{80,96},{96,112},{112,128},... | collective-permute-start | bytes 393224 | tf_op jit(solution)/shard_map/while/body/eval_jaxpr/ppermute | solution.py:12
  265.1 8.4 %collective-permute-start = (bf16[2,256,128]{2,1,0:T(8,128)(2,1)S(1)}, bf16[2,256,128]{2,1,0:T(8,128)(2,1)S(1)}, u32[]{:S(2)}, u32[]{:S(2)}) collective-permute-start(bf16[2,256,128]{2,1,0:T(8,128)(2,1)S(1)} %get-tuple-element.836), channel_id=1, source_target_pairs={{0,16},{16,32},{32,48},{48,64},{64,80},{80,96},{96,112},{112,128},... | collective-permute-start | bytes 393224 | tf_op jit(solution)/shard_map/while/body/eval_jaxpr/ppermute | solution.py:12
  276.3 8.4 %collective-permute-start = (bf16[2,256,128]{2,1,0:T(8,128)(2,1)S(1)}, bf16[2,256,128]{2,1,0:T(8,128)(2,1)S(1)}, u32[]{:S(2)}, u32[]{:S(2)}) collective-permute-start(bf16[2,256,128]{2,1,0:T(8,128)(2,1)S(1)} %get-tuple-element.836), channel_id=1, source_target_pairs={{0,16},{16,32},{32,48},{48,64},{64,80},{80,96},{96,112},{112,128},... | collective-permute-start | bytes 393224 | tf_op jit(solution)/shard_map/while/body/eval_jaxpr/ppermute | solution.py:12
  287.6 8.4 %collective-permute-start = (bf16[2,256,128]{2,1,0:T(8,128)(2,1)S(1)}, bf16[2,256,128]{2,1,0:T(8,128)(2,1)S(1)}, u32[]{:S(2)}, u32[]{:S(2)}) collective-permute-start(bf16[2,256,128]{2,1,0:T(8,128)(2,1)S(1)} %get-tuple-element.836), channel_id=1, source_target_pairs={{0,16},{16,32},{32,48},{48,64},{64,80},{80,96},{96,112},{112,128},... | collective-permute-start | bytes 393224 | tf_op jit(solution)/shard_map/while/body/eval_jaxpr/ppermute | solution.py:12
  298.9 8.4 %collective-permute-start = (bf16[2,256,128]{2,1,0:T(8,128)(2,1)S(1)}, bf16[2,256,128]{2,1,0:T(8,128)(2,1)S(1)}, u32[]{:S(2)}, u32[]{:S(2)}) collective-permute-start(bf16[2,256,128]{2,1,0:T(8,128)(2,1)S(1)} %get-tuple-element.836), channel_id=1, source_target_pairs={{0,16},{16,32},{32,48},{48,64},{64,80},{80,96},{96,112},{112,128},... | collective-permute-start | bytes 393224 | tf_op jit(solution)/shard_map/while/body/eval_jaxpr/ppermute | solution.py:12
  310.2 8.4 %collective-permute-start = (bf16[2,256,128]{2,1,0:T(8,128)(2,1)S(1)}, bf16[2,256,128]{2,1,0:T(8,128)(2,1)S(1)}, u32[]{:S(2)}, u32[]{:S(2)}) collective-permute-start(bf16[2,256,128]{2,1,0:T(8,128)(2,1)S(1)} %get-tuple-element.836), channel_id=1, source_target_pairs={{0,16},{16,32},{32,48},{48,64},{64,80},{80,96},{96,112},{112,128},... | collective-permute-start | bytes 393224 | tf_op jit(solution)/shard_map/while/body/eval_jaxpr/ppermute | solution.py:12
  321.4 8.4 %collective-permute-start = (bf16[2,256,128]{2,1,0:T(8,128)(2,1)S(1)}, bf16[2,256,128]{2,1,0:T(8,128)(2,1)S(1)}, u32[]{:S(2)}, u32[]{:S(2)}) collective-permute-start(bf16[2,256,128]{2,1,0:T(8,128)(2,1)S(1)} %get-tuple-element.836), channel_id=1, source_target_pairs={{0,16},{16,32},{32,48},{48,64},{64,80},{80,96},{96,112},{112,128},... | collective-permute-start | bytes 393224 | tf_op jit(solution)/shard_map/while/body/eval_jaxpr/ppermute | solution.py:12
  329.9 8.4 %collective-permute-start = (bf16[2,256,128]{2,1,0:T(8,128)(2,1)S(1)}, bf16[2,256,128]{2,1,0:T(8,128)(2,1)S(1)}, u32[]{:S(2)}, u32[]{:S(2)}) collective-permute-start(bf16[2,256,128]{2,1,0:T(8,128)(2,1)S(1)} %get-tuple-element.836), channel_id=1, source_target_pairs={{0,16},{16,32},{32,48},{48,64},{64,80},{80,96},{96,112},{112,128},... | collective-permute-start | bytes 393224 | tf_op jit(solution)/shard_map/while/body/eval_jaxpr/ppermute | solution.py:12
  341.1 8.4 %collective-permute-start = (bf16[2,256,128]{2,1,0:T(8,128)(2,1)S(1)}, bf16[2,256,128]{2,1,0:T(8,128)(2,1)S(1)}, u32[]{:S(2)}, u32[]{:S(2)}) collective-permute-start(bf16[2,256,128]{2,1,0:T(8,128)(2,1)S(1)} %get-tuple-element.836), channel_id=1, source_target_pairs={{0,16},{16,32},{32,48},{48,64},{64,80},{80,96},{96,112},{112,128},... | collective-permute-start | bytes 393224 | tf_op jit(solution)/shard_map/while/body/eval_jaxpr/ppermute | solution.py:12
  352.4 8.4 %collective-permute-start = (bf16[2,256,128]{2,1,0:T(8,128)(2,1)S(1)}, bf16[2,256,128]{2,1,0:T(8,128)(2,1)S(1)}, u32[]{:S(2)}, u32[]{:S(2)}) collective-permute-start(bf16[2,256,128]{2,1,0:T(8,128)(2,1)S(1)} %get-tuple-element.836), channel_id=1, source_target_pairs={{0,16},{16,32},{32,48},{48,64},{64,80},{80,96},{96,112},{112,128},... | collective-permute-start | bytes 393224 | tf_op jit(solution)/shard_map/while/body/eval_jaxpr/ppermute | solution.py:12
  363.7 8.4 %collective-permute-start = (bf16[2,256,128]{2,1,0:T(8,128)(2,1)S(1)}, bf16[2,256,128]{2,1,0:T(8,128)(2,1)S(1)}, u32[]{:S(2)}, u32[]{:S(2)}) collective-permute-start(bf16[2,256,128]{2,1,0:T(8,128)(2,1)S(1)} %get-tuple-element.836), channel_id=1, source_target_pairs={{0,16},{16,32},{32,48},{48,64},{64,80},{80,96},{96,112},{112,128},... | collective-permute-start | bytes 393224 | tf_op jit(solution)/shard_map/while/body/eval_jaxpr/ppermute | solution.py:12
  375.0 8.4 %collective-permute-start = (bf16[2,256,128]{2,1,0:T(8,128)(2,1)S(1)}, bf16[2,256,128]{2,1,0:T(8,128)(2,1)S(1)}, u32[]{:S(2)}, u32[]{:S(2)}) collective-permute-start(bf16[2,256,128]{2,1,0:T(8,128)(2,1)S(1)} %get-tuple-element.836), channel_id=1, source_target_pairs={{0,16},{16,32},{32,48},{48,64},{64,80},{80,96},{96,112},{112,128},... | collective-permute-start | bytes 393224 | tf_op jit(solution)/shard_map/while/body/eval_jaxpr/ppermute | solution.py:12
  383.4 8.4 %collective-permute-start = (bf16[2,256,128]{2,1,0:T(8,128)(2,1)S(1)}, bf16[2,256,128]{2,1,0:T(8,128)(2,1)S(1)}, u32[]{:S(2)}, u32[]{:S(2)}) collective-permute-start(bf16[2,256,128]{2,1,0:T(8,128)(2,1)S(1)} %get-tuple-element.836), channel_id=1, source_target_pairs={{0,16},{16,32},{32,48},{48,64},{64,80},{80,96},{96,112},{112,128},... | collective-permute-start | bytes 393224 | tf_op jit(solution)/shard_map/while/body/eval_jaxpr/ppermute | solution.py:12
  391.8 8.4 %collective-permute-start = (bf16[2,256,128]{2,1,0:T(8,128)(2,1)S(1)}, bf16[2,256,128]{2,1,0:T(8,128)(2,1)S(1)}, u32[]{:S(2)}, u32[]{:S(2)}) collective-permute-start(bf16[2,256,128]{2,1,0:T(8,128)(2,1)S(1)} %get-tuple-element.836), channel_id=1, source_target_pairs={{0,16},{16,32},{32,48},{48,64},{64,80},{80,96},{96,112},{112,128},... | collective-permute-start | bytes 393224 | tf_op jit(solution)/shard_map/while/body/eval_jaxpr/ppermute | solution.py:12
  403.1 8.4 %collective-permute-start = (bf16[2,256,128]{2,1,0:T(8,128)(2,1)S(1)}, bf16[2,256,128]{2,1,0:T(8,128)(2,1)S(1)}, u32[]{:S(2)}, u32[]{:S(2)}) collective-permute-start(bf16[2,256,128]{2,1,0:T(8,128)(2,1)S(1)} %get-tuple-element.836), channel_id=1, source_target_pairs={{0,16},{16,32},{32,48},{48,64},{64,80},{80,96},{96,112},{112,128},... | collective-permute-start | bytes 393224 | tf_op jit(solution)/shard_map/while/body/eval_jaxpr/ppermute | solution.py:12
  414.4 8.4 %collective-permute-start = (bf16[2,256,128]{2,1,0:T(8,128)(2,1)S(1)}, bf16[2,256,128]{2,1,0:T(8,128)(2,1)S(1)}, u32[]{:S(2)}, u32[]{:S(2)}) collective-permute-start(bf16[2,256,128]{2,1,0:T(8,128)(2,1)S(1)} %get-tuple-element.836), channel_id=1, source_target_pairs={{0,16},{16,32},{32,48},{48,64},{64,80},{80,96},{96,112},{112,128},... | collective-permute-start | bytes 393224 | tf_op jit(solution)/shard_map/while/body/eval_jaxpr/ppermute | solution.py:12
  (6 other events, 530.2 us)
Sparse Core Ops, SparseCore 0:
  51.2 58.7 all-gather.2
  113.0 62.2 all-gather.4
where the time goes:
time: 507 us; the launch traced here: 504 us
  waiting for transfers between devices  154 us (30%)
  blocking collectives  77.7 us (15%)
  loops' own time  70.4 us (14%)
  matrix products  67.3 us (13%)
  starting transfers between devices  60.1 us (12%)
  local copies, waits for them, and re-layouts  34.8 us (7%)
  other arithmetic  22.4 us (4%)
  between operations  17.1 us (3%)
    ppermute x31, waiting for transfers between devices, shifted(): return lax.ppermute(value, axis, pairs)  154 us
    ppermute x31, starting transfers between devices, shifted(): return lax.ppermute(value, axis, pairs)  60 us
    all_gather x1, blocking collectives, per_device(): lax.all_gather(frame_k, 'seq', axis=1, tiled=True)  43.8 us
    another operation x1, loops' own time, per_device(): running, _ = lax.fori_loop(1, seq_count, one_hop, (running, stacked_own))  42.9 us
    dot_general x33, matrix products, attend_tile(): jnp.einsum('thk,kd->thd', weights.astype(jnp.bfloat16), value_rows, prefe...  42.6 us
    all_gather x1, blocking collectives, per_device(): lax.all_gather(frame_v, 'seq', axis=1, tiled=True)  34 us
    dot_general x33, matrix products, attend_tile(): jnp.einsum('thd,kd->thk', queries, key_rows, preferred_element_type=jnp.f...  24.7 us
    dynamic_slice x32, local copies, waits for them, and re-layouts, self_tile(): source_block = block_pos[source]  19.8 us
  transfers between devices with their start and end apart: 33, of which 31 were waited for; matrix products, arithmetic and copies ran while one was open for 15% of the time, Pallas kernels for 0%

commit v1 on v0

v1 whole, which is shorter than its diff:
```python
import jax
import jax.numpy as jnp
from jax import lax
from jax.experimental import pallas as pl
from jax.experimental.pallas import tpu as pltpu
from jax.sharding import PartitionSpec as P

H = 8
DH = 128
ROWS = 256
ONES = 16
FACTOR = DH**-0.5
FACTOR2 = FACTOR * 1.4426950408889634
LOW, HIGH = 1e-28, 1e28
F32, BF16 = jnp.float32, jnp.bfloat16

Y, Z, CORES = 2, 8, 2
YH, X = 4, 4


def seq_id(y, z, c):
    return (y % Y * Z + z % Z) * CORES + c % CORES


ZC_GROUPS = [[seq_id(y, z, c) for z in range(Z) for c in range(CORES)] for y in range(Y)]
YZ_GROUPS = [[seq_id(y, z, c) for y in range(Y) for z in range(Z)] for c in range(CORES)]
YH_GROUPS = [[y * X + x for y in range(YH)] for x in range(X)]
TO_Y = [(seq_id(y, z, c), seq_id(y + 1, z, c)) for y in range(Y) for z in range(Z) for c in range(CORES)]
TO_CORE = [(seq_id(y, z, c), seq_id(y, z, c + 1)) for y in range(Y) for z in range(Z) for c in range(CORES)]


def to_x(steps):
    return [(y * X + x, y * X + (x + steps) % X) for y in range(YH) for x in range(X)]


def dot(a, b):
    return lax.dot_general(a, b, (((1,), (0,)), ((), ())), preferred_element_type=F32)


def causal():
    keys = lax.broadcasted_iota(jnp.int32, (ROWS, ROWS), 0)
    queries = lax.broadcasted_iota(jnp.int32, (ROWS, ROWS), 1)
    return keys <= queries


def add_keys(qt, acc, keys, values, masked=False, depth=2):
    ones = jnp.ones((ONES, keys.shape[0]), BF16)
    weights = jnp.concatenate([values.T, ones], axis=0)
    scores = [dot(keys, qt[h]) for h in range(depth)]
    for h in range(H):
        p = jnp.exp2(scores.pop(0) * FACTOR2)
        if masked:
            p = jnp.where(causal(), p, 0.0)
        p = p.astype(BF16)
        if h + depth < H:
            scores.append(dot(keys, qt[h + depth]))
        acc[h] += dot(weights, p)


def safe_attention(qt, acc, top, read, parts, own):
    acc[...] = jnp.zeros_like(acc)

    def scores_of(keys, h, masked):
        s = dot(keys, qt[h]) * FACTOR
        return jnp.where(causal(), s, -1e30) if masked else s

    def find(keys, masked):
        def head(h, _):
            s = scores_of(keys, h, masked)
            top[h] = jnp.maximum(top[h], jnp.max(s, axis=0, keepdims=True))
            return 0

        lax.fori_loop(0, H, head, 0)

    def add(keys, values, masked):
        weights = jnp.concatenate([values.T, jnp.ones((ONES, keys.shape[0]), BF16)], axis=0)

        def head(h, _):
            p = jnp.exp(scores_of(keys, h, masked) - top[h])
            acc[h] += dot(weights, p.astype(BF16))
            return 0

        lax.fori_loop(0, H, head, 0)

    top[...] = jnp.full_like(top, -1e30)

    def first(j, _):
        find(read(j)[0], False)
        return 0

    def second(j, _):
        add(*read(j), False)
        return 0

    lax.fori_loop(0, parts, first, 0)
    if own is not None:
        find(own[0][...], True)
    lax.fori_loop(0, parts, second, 0)
    if own is not None:
        add(own[0][...], own[1][...], True)


def run(q_ref, o_ref, qt, acc, top, chosen, parts, read, group, own):
    for h in range(H):
        qt[h] = q_ref[:, h * DH : (h + 1) * DH].T
    acc[...] = jnp.zeros_like(acc)

    def several(first, number):
        pairs = [read(chosen[first + i]) for i in range(number)]
        return tuple(jnp.concatenate(x, axis=0) for x in zip(*pairs))

    def whole(i, _):
        add_keys(qt, acc, *several(i * group, group))
        return 0

    if own is not None:
        add_keys(qt, acc, own[0][...], own[1][...], masked=True, depth=4)
    lax.fori_loop(0, parts // group, whole, 0)
    size = group // 2
    while size:
        @pl.when(parts // size % 2 == 1)
        def _(size=size):
            add_keys(qt, acc, *several(parts // (2 * size) * (2 * size), size), depth=4)

        size //= 2

    sums = acc[:, DH : DH + 1, :]
    good = jnp.logical_and(sums > LOW, sums < HIGH)
    worst = jnp.min(jnp.where(good, 1.0, 0.0))

    @pl.when(worst < 0.5)
    def _():
        safe_attention(qt, acc, top, lambda j: read(chosen[j]), parts, own)

    for h in range(H):
        o_ref[:, h * DH : (h + 1) * DH] = (acc[h, :DH] / acc[h, DH : DH + 1]).astype(BF16).T


def self_kernel(place, block_pos, q_ref, kv, o_ref, qt, acc, top, chosen):
    me = place[0]
    mine = block_pos[me]
    my_y, my_zc = me // (Z * CORES), me % (Z * CORES)

    def listed(i, count):
        zc, other = i // Y, i % Y
        source = (my_y + other) % Y * (Z * CORES) + zc
        keep = block_pos[source] < mine

        @pl.when(keep)
        def _():
            chosen[count] = i

        return count + keep.astype(jnp.int32)

    parts = lax.fori_loop(0, Y * Z * CORES, listed, 0)

    def read(i):
        return kv[i // Y, i % Y, 0], kv[i // Y, i % Y, 1]

    run(q_ref, o_ref, qt, acc, top, chosen, parts, read, 4, (kv.at[my_zc, 0, 0], kv.at[my_zc, 0, 1]))


def cross_kernel(place, block_pos, mask, q_ref, mine_ref, other_ref, o_ref, qt, acc, top, chosen):
    row = block_pos[place[0]]
    my_x = place[1] % X

    def listed(i, count):
        slot, y = i // YH, i % YH
        shift = jnp.where(slot == 0, 0, jnp.where(slot == 1, X - 1, jnp.where(slot == 2, 1, 2)))
        keep = mask[row, y * X + (my_x + shift) % X] > 0

        @pl.when(keep)
        def _():
            chosen[count] = i

        return count + keep.astype(jnp.int32)

    parts = lax.fori_loop(0, X * YH, listed, 0)

    def read(i):
        halves = [ref[i // YH, i % YH] for ref in (mine_ref, other_ref)]
        return tuple(
            jnp.concatenate([half[:, which].reshape(-1, DH) for half in halves], axis=0) for which in (0, 1)
        )

    run(q_ref, o_ref, qt, acc, top, chosen, parts, read, 2, None)


def call(kernel, name, scalars, arrays, parts):
    return pl.pallas_call(
        kernel,
        out_shape=jax.ShapeDtypeStruct((ROWS, H * DH), BF16),
        in_specs=[pl.BlockSpec(memory_space=pltpu.SMEM)] * len(scalars)
        + [pl.BlockSpec(memory_space=pltpu.VMEM)] * len(arrays),
        out_specs=pl.BlockSpec(memory_space=pltpu.VMEM),
        scratch_shapes=[
            pltpu.VMEM((H, DH, ROWS), BF16),
            pltpu.VMEM((H, DH + ONES, ROWS), F32),
            pltpu.VMEM((H, 1, ROWS), F32),
            pltpu.SMEM((parts,), jnp.int32),
        ],
        compiler_params=pltpu.CompilerParams(vmem_limit_bytes=40 * 2**20),
        cost_estimate=pl.CostEstimate(
            flops=16 * 4 * H * ROWS * ROWS * DH, bytes_accessed=6 * 2**20, transcendentals=16 * H * ROWS * ROWS
        ),
        name=name,
    )(*scalars, *arrays)


def per_device(text_q, cross_q, text_k, text_v, frame_k, frame_v, block_pos, frame_mask):
    place = jnp.stack([lax.axis_index("seq"), lax.axis_index("grp")]).astype(jnp.int32)

    own = jnp.stack([text_k[0], text_v[0]])
    across = lax.ppermute(own, "seq", TO_Y)
    text = lax.all_gather(jnp.stack([own, across]), "seq", axis_index_groups=ZC_GROUPS)

    piece = jnp.stack([frame_k[0], frame_v[0]])
    frame = lax.all_to_all(
        jnp.broadcast_to(piece, (Y * Z, *piece.shape)), "seq", 0, 0, axis_index_groups=YZ_GROUPS
    )
    column = lax.all_to_all(jnp.broadcast_to(frame, (YH, *frame.shape)), "grp", 0, 0, axis_index_groups=YH_GROUPS)
    columns = [column] + [lax.ppermute(column, "grp", to_x(steps)) for steps in (1, -1, 2)]
    half = jnp.stack(columns)
    other_half = lax.ppermute(half, "seq", TO_CORE)

    cross_out = call(
        cross_kernel, "cross", [place, block_pos, frame_mask], [cross_q[0], half, other_half], X * YH
    )
    self_out = call(self_kernel, "own", [place, block_pos], [text_q[0], text], Y * Z * CORES)
    return self_out[None], cross_out[None]


def solution(mesh):
    rows = P("grp", "seq", None)
    return jax.shard_map(
        per_device,
        mesh=mesh,
        in_specs=(rows, rows, rows, rows, rows, rows, P(), P()),
        out_specs=(rows, rows),
        check_vma=False,
    )
```

time: 507 us -> 301 us (0.59)
  the two profiles are of different devices: /device:TPU:18 before, /device:TPU:385 now
where the time goes in v1:
time: 301 us; the launch traced here: 300 us
  Pallas kernels  207 us (69%)
  blocking collectives  28.1 us (9%)
  waiting for transfers between devices  27.7 us (9%)
  starting transfers between devices  17.6 us (6%)
  between operations  14.1 us (5%)
  local copies, waits for them, and re-layouts  4.07 us (1%)
    pallas_call x2, Pallas kernels, call(): pl.pallas_call(kernel, out_shape=jax.ShapeDtypeStruct((ROWS, H * DH), BF1...  207 us
    ppermute x3, waiting for transfers between devices, per_device(): lax.ppermute(column, 'grp', to_x(steps))  20.9 us
    all_to_all x1, blocking collectives, per_device(): lax.all_to_all(jnp.broadcast_to(frame, (YH, *frame.shape)), 'grp', 0, 0,...  17.4 us
    all_to_all x1, blocking collectives, per_device(): lax.all_to_all(jnp.broadcast_to(piece, (Y * Z, *piece.shape)), 'seq', 0,...  10.7 us
    ppermute x3, starting transfers between devices, per_device(): lax.ppermute(column, 'grp', to_x(steps))  9.32 us
  transfers between devices with their start and end apart: 6, of which 5 were waited for; matrix products, arithmetic and copies ran while one was open for 0% of the time, Pallas kernels for 18%

profile of v1, /device:TPU:385, one launch (start us, length us, event | category | flops | bytes accessed | tf_op | source)
XLA Modules:
  0.0 300.1 jit_solution(6825195975386193462)
XLA Ops:
  7.2 0.0 all-gather.3.cloned.1.call-start
  7.2 0.8 constant_dynamic-update-slice_fusion.1
  8.1 0.9 constant_dynamic-update-slice_fusion
  8.9 3.2 %collective-permute-start = (bf16[2,256,128]{2,1,0:T(8,128)(2,1)S(1)}, bf16[2,256,128]{2,1,0:T(8,128)(2,1)S(1)}, u32[]{:S(2)}, u32[]{:S(2)}) collective-permute-start(bf16[2,256,128]{2,1,0:T(8,128)(2,1)S(1)} %constant_dynamic-update-slice_fusion), channel_id=1, source_target_pairs={{0,256},{16,272},{32,288},{48,304},{64,320},{80,336},{96,352},{112... | collective-permute-start | bytes 393224 | tf_op jit(solution)/shard_map/ppermute | solution.py:214
  12.1 3.0 %collective-permute-done = bf16[2,256,128]{2,1,0:T(8,128)(2,1)S(1)} collective-permute-done((bf16[2,256,128]{2,1,0:T(8,128)(2,1)S(1)}, bf16[2,256,128]{2,1,0:T(8,128)(2,1)S(1)}, u32[]{:S(2)}, u32[]{:S(2)}) %collective-permute-start) | collective-permute-done | bytes 131104 | tf_op jit(solution)/shard_map/ppermute | solution.py:214
  15.2 0.7 pad_maximum_fusion.1
  15.9 0.0 all-gather.3.cloned.1.call-update
  15.9 0.7 pad_maximum_fusion.2
  16.6 10.7 %all_to_all.10 = bf16[16,2,16,128]{3,2,1,0:T(8,128)(2,1)S(1)} all-to-all(bf16[16,2,16,128]{3,2,1,0:T(8,128)(2,1)S(1)} %broadcast_in_dim.13), channel_id=1, replica_groups={{0,32,64,96,128,160,192,224,256,288,320,352,384,416,448,480},{16,48,80,..., dimensions={0} | all-to-all | bytes 262144 | tf_op jit(solution)/shard_map/all_to_all | solution.py:218
  27.3 0.1 broadcast_in_dim.14
  27.4 17.4 %all_to_all.11 = bf16[4,16,2,16,128]{4,3,2,1,0:T(8,128)(2,1)S(1)} all-to-all(bf16[4,16,2,16,128]{4,3,2,1,0:T(8,128)(2,1)S(1)} %broadcast_in_dim.14), channel_id=1, replica_groups={{0,4,8,12},{1,5,9,13},{2,6,10,14},{3,7,11,15},{16,20,24,28},{17,21,25,2..., dimensions={0} | all-to-all | bytes 1048576 | tf_op jit(solution)/shard_map/all_to_all | solution.py:221
  44.8 4.4 %collective-permute-start.2 = (bf16[4,16,2,16,128]{4,3,2,1,0:T(8,128)(2,1)S(1)}, bf16[4,16,2,16,128]{4,3,2,1,0:T(8,128)(2,1)S(1)}, u32[]{:S(2)}, u32[]{:S(2)}) collective-permute-start(bf16[4,16,2,16,128]{4,3,2,1,0:T(8,128)(2,1)S(1)} %all_to_all.11), channel_id=1, source_target_pairs={{0,3},{1,0},{2,1},{3,2},{4,7},{5,4},{6,5},{7,6},{8,11},{9,8},{10,9... | collective-permute-start | bytes 1572872 | tf_op jit(solution)/shard_map/ppermute | solution.py:222
  49.2 2.4 collective-permute-start.3
  51.6 2.5 collective-permute-start.1
  54.1 4.2 %collective-permute-done.2 = bf16[4,16,2,16,128]{4,3,2,1,0:T(8,128)(2,1)S(1)} collective-permute-done((bf16[4,16,2,16,128]{4,3,2,1,0:T(8,128)(2,1)S(1)}, bf16[4,16,2,16,128]{4,3,2,1,0:T(8,128)(2,1)S(1)}, u32[]{:S(2)}, u32[]{:S(2)}) %collective-permute-start.2) | collective-permute-done | bytes 524320 | tf_op jit(solution)/shard_map/ppermute | solution.py:222
  58.4 2.4 collective-permute-done.3
  60.7 14.3 %collective-permute-done.1 = bf16[4,16,2,16,128]{4,3,2,1,0:T(8,128)(2,1)S(1)} collective-permute-done((bf16[4,16,2,16,128]{4,3,2,1,0:T(8,128)(2,1)S(1)}, bf16[4,16,2,16,128]{4,3,2,1,0:T(8,128)(2,1)S(1)}, u32[]{:S(2)}, u32[]{:S(2)}) %collective-permute-start.1) | collective-permute-done | bytes 524320 | tf_op jit(solution)/shard_map/ppermute | solution.py:222
  75.0 0.0 copy-start.4
  75.0 0.0 copy-start.1
  75.0 0.0 copy-start.3
  75.0 0.3 pad_maximum_fusion.mine_ref
  75.3 5.0 %collective-permute-start.4 = (bf16[4,4,16,2,16,128]{5,4,3,2,1,0:T(8,128)(2,1)S(1)}, bf16[4,4,16,2,16,128]{5,4,3,2,1,0:T(8,128)(2,1)}, u32[]{:S(2)}, u32[]{:S(2)}) collective-permute-start(bf16[4,4,16,2,16,128]{5,4,3,2,1,0:T(8,128)(2,1)S(1)} %pad_maximum_fusion.mine_ref), channel_id=1, source_target_pairs={{0,16},{16,0},{32,48},{48,32},{64,80},{80,64},{96,112},{112,96},{1... | collective-permute-start | bytes 6291464 | tf_op jit(solution)/shard_map/ppermute | solution.py:224
  80.3 0.0 copy-done.4
  80.4 0.1 copy.11.mask
  80.4 0.1 pad_add_fusion.place
  80.5 3.7 %collective-permute-done.4.other_ref = bf16[4,4,16,2,16,128]{5,4,3,2,1,0:T(8,128)(2,1)} collective-permute-done((bf16[4,4,16,2,16,128]{5,4,3,2,1,0:T(8,128)(2,1)S(1)}, bf16[4,4,16,2,16,128]{5,4,3,2,1,0:T(8,128)(2,1)}, u32[]{:S(2)}, u32[]{:S(2)}) %collective-permute-start.4) | collective-permute-done | bytes 2097184 | tf_op jit(solution)/shard_map/ppermute | solution.py:224
  84.2 0.0 copy-done.1
  84.2 0.0 copy-done.3
  84.2 54.6 %cross.1 = bf16[256,1024]{1,0:T(8,128)(2,1)} custom-call(s32[2]{0:T(128)S(1)} %pad_add_fusion.place, s32[32]{0:T(128)S(1)} %copy-done.3, s32[32,16]{1,0:T(8,128)S(1)} %copy.11.mask, bf16[256,1024]{1,0:T(8,128)(2,1)S(1)} %bitcast.14, bf16[4,4,16,2,16,128]{5,4,3,2,1,0:T(8,128)(2,1)S(1)} %pad_maximum_fusion.mine_ref, ...), custom_call_target="tpu_custom_call" | custom-call | flops 4294967296 | bytes 6291456 | tf_op jit(solution)/shard_map/cross/pallas_call | solution.py:190
  138.8 0.0 copy-done.2
  138.8 2.2 copy-done
  141.0 152.3 %own.1 = bf16[256,1024]{1,0:T(8,128)(2,1)} custom-call(s32[2]{0:T(128)S(1)} %pad_add_fusion.place, s32[32]{0:T(128)S(1)} %copy-done.3, bf16[256,1024]{1,0:T(8,128)(2,1)S(1)} %bitcast.15, bf16[16,2,2,256,128]{4,3,2,1,0:T(8,128)(2,1)S(1)} %bitcast.13), custom_call_target="tpu_custom_call" | custom-call | flops 4294967296 | bytes 6291456 | tf_op jit(solution)/shard_map/own/pallas_call | solution.py:190
  (4 shorter events, 0.0 us)
Async XLA Ops:
  7.2 131.7 %all-gather.3.cloned.1.call-start = ((), (), s32[]{:S(2)}) async-start(), calls=%async_computation.2 | async-start | bytes 4456448 | tf_op jit(solution)/shard_map/all_gather | solution.py:215
  8.9 6.3 %collective-permute-start = (bf16[2,256,128]{2,1,0:T(8,128)(2,1)S(1)}, bf16[2,256,128]{2,1,0:T(8,128)(2,1)S(1)}, u32[]{:S(2)}, u32[]{:S(2)}) collective-permute-start(bf16[2,256,128]{2,1,0:T(8,128)(2,1)S(1)} %constant_dynamic-update-slice_fusion), channel_id=1, source_target_pairs={{0,256},{16,272},{32,288},{48,304},{64,320},{80,336},{96,352},{112... | collective-permute-start | bytes 393224 | tf_op jit(solution)/shard_map/ppermute | solution.py:214
  44.8 13.6 %collective-permute-start.2 = (bf16[4,16,2,16,128]{4,3,2,1,0:T(8,128)(2,1)S(1)}, bf16[4,16,2,16,128]{4,3,2,1,0:T(8,128)(2,1)S(1)}, u32[]{:S(2)}, u32[]{:S(2)}) collective-permute-start(bf16[4,16,2,16,128]{4,3,2,1,0:T(8,128)(2,1)S(1)} %all_to_all.11), channel_id=1, source_target_pairs={{0,3},{1,0},{2,1},{3,2},{4,7},{5,4},{6,5},{7,6},{8,11},{9,8},{10,9... | collective-permute-start | bytes 1572872 | tf_op jit(solution)/shard_map/ppermute | solution.py:222
  49.2 11.5 %collective-permute-start.3 = (bf16[4,16,2,16,128]{4,3,2,1,0:T(8,128)(2,1)S(1)}, bf16[4,16,2,16,128]{4,3,2,1,0:T(8,128)(2,1)S(1)}, u32[]{:S(2)}, u32[]{:S(2)}) collective-permute-start(bf16[4,16,2,16,128]{4,3,2,1,0:T(8,128)(2,1)S(1)} %all_to_all.11), channel_id=1, source_target_pairs={{0,2},{1,3},{2,0},{3,1},{4,6},{5,7},{6,4},{7,5},{8,10},{9,11},{10,... | collective-permute-start | bytes 1572872 | tf_op jit(solution)/shard_map/ppermute | solution.py:222
  51.6 23.4 %collective-permute-start.1 = (bf16[4,16,2,16,128]{4,3,2,1,0:T(8,128)(2,1)S(1)}, bf16[4,16,2,16,128]{4,3,2,1,0:T(8,128)(2,1)S(1)}, u32[]{:S(2)}, u32[]{:S(2)}) collective-permute-start(bf16[4,16,2,16,128]{4,3,2,1,0:T(8,128)(2,1)S(1)} %all_to_all.11), channel_id=1, source_target_pairs={{0,1},{1,2},{2,3},{3,0},{4,5},{5,6},{6,7},{7,4},{8,9},{9,10},{10,1... | collective-permute-start | bytes 1572872 | tf_op jit(solution)/shard_map/ppermute | solution.py:222
  75.0 5.3 %copy-start.4 = (s32[32,16]{0,1:T(8,128)S(1)}, s32[32,16]{0,1:T(8,128)}, u32[]{:S(2)}) copy-start(s32[32,16]{0,1:T(8,128)} %param.15) | copy-start | bytes 6148
  75.0 9.2 %copy-start.1 = (bf16[1,256,1024]{2,1,0:T(8,128)(2,1)S(1)}, bf16[1,256,1024]{2,1,0:T(8,128)(2,1)}, u32[]{:S(2)}) copy-start(bf16[1,256,1024]{2,1,0:T(8,128)(2,1)} %param.9) | copy-start | bytes 1572868
  75.0 9.2 %copy-start.3 = (s32[32]{0:T(128)S(1)}, s32[32]{0:T(128)}, u32[]{:S(2)}) copy-start(s32[32]{0:T(128)} %block_pos.3) | copy-start | bytes 388
  75.3 9.0 %collective-permute-start.4 = (bf16[4,4,16,2,16,128]{5,4,3,2,1,0:T(8,128)(2,1)S(1)}, bf16[4,4,16,2,16,128]{5,4,3,2,1,0:T(8,128)(2,1)}, u32[]{:S(2)}, u32[]{:S(2)}) collective-permute-start(bf16[4,4,16,2,16,128]{5,4,3,2,1,0:T(8,128)(2,1)S(1)} %pad_maximum_fusion.mine_ref), channel_id=1, source_target_pairs={{0,16},{16,0},{32,48},{48,32},{64,80},{80,64},{96,112},{112,96},{1... | collective-permute-start | bytes 6291464 | tf_op jit(solution)/shard_map/ppermute | solution.py:224
  84.2 54.6 %copy-start.2 = (bf16[1,256,1024]{2,1,0:T(8,128)(2,1)S(1)}, bf16[1,256,1024]{2,1,0:T(8,128)(2,1)}, u32[]{:S(2)}) copy-start(bf16[1,256,1024]{2,1,0:T(8,128)(2,1)} %param.8) | copy-start | bytes 1572868
  138.8 2.2 copy-start
Sparse Core Ops, SparseCore 0:
  16.0 44.3 all-gather.2

commit v2 on v1

v2 whole, which is shorter than its diff:
```python
import functools

import jax
import jax.numpy as jnp
from jax import lax
from jax.experimental import pallas as pl
from jax.experimental.pallas import tpu as pltpu
from jax.sharding import PartitionSpec as P

H = 8
DH = 128
ROWS = 256
ONES = 16
FACTOR = DH**-0.5
FACTOR2 = FACTOR * 1.4426950408889634
LOW, HIGH = 1e-28, 1e28
F32, BF16 = jnp.float32, jnp.bfloat16

Y, Z, CORES = 2, 8, 2
YH, X = 4, 4
GROUP = 4
COLUMN_SHIFTS = (0, -1, 1, 2)


def seq_id(y, z, c):
    return (y % Y * Z + z % Z) * CORES + c % CORES


Z_GROUPS = [[seq_id(y, z, c) for z in range(Z)] for y in range(Y) for c in range(CORES)]
PLANE_GROUPS = [
    [(yh * X + x) * (Y * Z * CORES) + seq_id(y, z, c) for yh in range(YH) for y in range(Y) for z in range(Z)]
    for x in range(X)
    for c in range(CORES)
]
TO_Y = [(seq_id(y, z, c), seq_id(y + 1, z, c)) for y in range(Y) for z in range(Z) for c in range(CORES)]
TO_CORE = [(seq_id(y, z, c), seq_id(y, z, c + 1)) for y in range(Y) for z in range(Z) for c in range(CORES)]


def to_x(steps):
    return [(y * X + x, y * X + (x + steps) % X) for y in range(YH) for x in range(X)]


def dot(a, b):
    return lax.dot_general(a, b, (((1,), (0,)), ((), ())), preferred_element_type=F32)


def causal():
    keys = lax.broadcasted_iota(jnp.int32, (ROWS, ROWS), 0)
    queries = lax.broadcasted_iota(jnp.int32, (ROWS, ROWS), 1)
    return keys <= queries


def weights_of(values):
    return jnp.concatenate([values.T, jnp.ones((ONES, values.shape[0]), BF16)], axis=0)


def add_keys(qt, acc, keys, values, masked=False, depth=2):
    weights = weights_of(values)
    scores = [dot(keys, qt[h]) for h in range(depth)]
    for h in range(H):
        p = jnp.exp2(scores.pop(0) * FACTOR2)
        if masked:
            p = jnp.where(causal(), p, 0.0)
        p = p.astype(BF16)
        if h + depth < H:
            scores.append(dot(keys, qt[h + depth]))
        acc[h] += dot(weights, p)


def safe_attention(qt, acc, top, read, parts, own):
    acc[...] = jnp.zeros_like(acc)
    top[...] = jnp.full_like(top, -1e30)

    def scores_of(keys, h, masked):
        s = dot(keys, qt[h]) * FACTOR
        return jnp.where(causal(), s, -1e30) if masked else s

    def find(keys, values, masked):
        def head(h, _):
            s = scores_of(keys, h, masked)
            top[h] = jnp.maximum(top[h], jnp.max(s, axis=0, keepdims=True))
            return 0

        lax.fori_loop(0, H, head, 0)

    def add(keys, values, masked):
        weights = weights_of(values)

        def head(h, _):
            p = jnp.exp(scores_of(keys, h, masked) - top[h])
            acc[h] += dot(weights, p.astype(BF16))
            return 0

        lax.fori_loop(0, H, head, 0)

    for visit in (find, add):
        def one(j, _, visit=visit):
            visit(*read(j, 1), False)
            return 0

        lax.fori_loop(0, parts, one, 0)
        if own is not None:
            visit(own[0][...], own[1][...], True)


def attend(q_ref, acc, qt, top, parts, read, own):
    for h in range(H):
        qt[h] = q_ref[:, h * DH : (h + 1) * DH].T
    acc[...] = jnp.zeros_like(acc)
    top[...] = jnp.zeros_like(top)
    if own is not None:
        add_keys(qt, acc, own[0][...], own[1][...], masked=True, depth=4)

    def whole(i, _):
        add_keys(qt, acc, *read(i * GROUP, GROUP))
        return 0

    lax.fori_loop(0, parts // GROUP, whole, 0)
    size = GROUP // 2
    while size:
        @pl.when(parts // size % 2 == 1)
        def _(size=size):
            add_keys(qt, acc, *read(parts // (2 * size) * (2 * size), size), depth=4)

        size //= 2

    if own is None:
        @pl.when(parts == 0)
        def _():
            top[...] = jnp.full_like(top, -1e30)

    sums = acc[:, DH : DH + 1, :]
    good = jnp.logical_and(sums > LOW, sums < HIGH)
    worst = jnp.min(jnp.where(good, 1.0, 0.0))
    some = parts >= (1 if own is None else 0)

    @pl.when(jnp.logical_and(worst < 0.5, some))
    def _():
        safe_attention(qt, acc, top, read, parts, own)

    for h in range(H):
        acc[h, DH + ONES // 2 :] = jnp.broadcast_to(top[h], (ONES // 2, ROWS))


def list_blocks(place, block_pos, chosen, rows_of):
    me = place[0]
    my_y, my_core = me // (Z * CORES), me % CORES

    def listed(i, count):
        source = (my_y + i % Y) % Y * (Z * CORES) + i // Y * CORES + my_core
        keep = block_pos[source] < block_pos[rows_of]

        @pl.when(keep)
        def _():
            chosen[count] = i

        return count + keep.astype(jnp.int32)

    return lax.fori_loop(0, Y * Z, listed, 0)


def self_kernel(place, block_pos, q_ref, partner_ref, kv, mine, theirs, qt, top, chosen):
    def read(first, number):
        blocks = [chosen[first + i] for i in range(number)]
        return tuple(jnp.concatenate([kv[b // Y, b % Y, which] for b in blocks], axis=0) for which in (0, 1))

    me = place[0]
    partner = me + 1 - 2 * (me % CORES)
    attend(partner_ref, theirs, qt, top, list_blocks(place, block_pos, chosen, partner), read, None)
    my_z = me // CORES % Z
    own = (kv.at[my_z, 0, 0], kv.at[my_z, 0, 1])
    attend(q_ref, mine, qt, top, list_blocks(place, block_pos, chosen, me), read, own)


def cross_kernel(partner, place, block_pos, mask, q_ref, *refs):
    columns, (out, qt, top, keys, values) = refs[:X], refs[X:]
    me = place[0]
    row = block_pos[me + 1 - 2 * (me % CORES) if partner else me]
    my_x = place[1] % X
    parts = jnp.int32(0)
    for column, shift in zip(columns, COLUMN_SHIFTS):
        for y in range(YH):
            keep = mask[row, y * X + (my_x + shift) % X] > 0

            @pl.when(keep)
            def _(column=column, y=y, parts=parts):
                at = pl.ds(pl.multiple_of(parts * ROWS, ROWS), ROWS)
                keys[at] = column[y, :, 0].reshape(ROWS, DH)
                values[at] = column[y, :, 1].reshape(ROWS, DH)

            parts = parts + keep.astype(jnp.int32)

    def read(first, number):
        at = pl.ds(pl.multiple_of(first * ROWS, ROWS), number * ROWS)
        return keys[at], values[at]

    attend(q_ref, out, qt, top, parts, read, None)


def join_kernel(mine, theirs, o_ref):
    for h in range(H):
        shifts = [part[h, DH + ONES // 2 : DH + ONES // 2 + 1] for part in (mine, theirs)]
        common = jnp.maximum(*shifts)
        scales = [jnp.exp(shift - common) for shift in shifts]
        total = sum(part[h, DH : DH + 1] * scale for part, scale in zip((mine, theirs), scales))
        rows = sum(part[h, :DH] * (scale / total) for part, scale in zip((mine, theirs), scales))
        o_ref[:, h * DH : (h + 1) * DH] = rows.astype(BF16).T


SUMS = jax.ShapeDtypeStruct((H, DH + ONES, ROWS), F32)
WORK = [pltpu.VMEM((H, DH, ROWS), BF16), pltpu.VMEM((H, 1, ROWS), F32)]


def call(kernel, name, scalars, arrays, outs, scratch, units):
    return pl.pallas_call(
        kernel,
        out_shape=outs,
        in_specs=[pl.BlockSpec(memory_space=pltpu.SMEM)] * len(scalars)
        + [pl.BlockSpec(memory_space=pltpu.VMEM)] * len(arrays),
        out_specs=jax.tree.map(lambda _: pl.BlockSpec(memory_space=pltpu.VMEM), outs),
        scratch_shapes=scratch,
        compiler_params=pltpu.CompilerParams(vmem_limit_bytes=32 * 2**20),
        cost_estimate=pl.CostEstimate(
            flops=units * 8 * H * ROWS * ROWS * DH, bytes_accessed=4 * 2**20, transcendentals=units * H * ROWS * ROWS
        ),
        name=name,
    )(*scalars, *arrays)


def per_device(text_q, cross_q, text_k, text_v, frame_k, frame_v, block_pos, frame_mask):
    place = jnp.stack([lax.axis_index("seq"), lax.axis_index("grp")]).astype(jnp.int32)

    own = jnp.stack([text_k[0], text_v[0]])
    across = lax.ppermute(own, "seq", TO_Y)
    partner_q = lax.ppermute(text_q[0], "seq", TO_CORE)
    partner_cross_q = lax.ppermute(cross_q[0], "seq", TO_CORE)
    text = lax.all_gather(jnp.stack([own, across]), "seq", axis_index_groups=Z_GROUPS)

    piece = jnp.stack([frame_k[0], frame_v[0]])
    plane = lax.all_to_all(
        jnp.broadcast_to(piece, (YH * Y * Z, *piece.shape)), ("grp", "seq"), 0, 0, axis_index_groups=PLANE_GROUPS
    )
    column = plane.reshape(YH, Y * Z, *piece.shape)
    columns = [column] + [lax.ppermute(column, "grp", to_x(-shift)) for shift in COLUMN_SHIFTS[1:]]

    mine, theirs = call(
        self_kernel, "own", [place, block_pos], [text_q[0], partner_q, text], (SUMS, SUMS),
        [*WORK, pltpu.SMEM((Y * Z,), jnp.int32)], 16,
    )
    self_theirs = lax.ppermute(theirs, "seq", TO_CORE)

    def cross(queries, partner):
        return call(
            functools.partial(cross_kernel, partner), "cross", [place, block_pos, frame_mask], [queries, *columns],
            SUMS, [*WORK, *[pltpu.VMEM((X * YH * ROWS, DH), BF16)] * 2], 5,
        )

    partner_cross_q, mine = lax.optimization_barrier((partner_cross_q, mine))
    cross_theirs = cross(partner_cross_q, True)
    own_cross_q, cross_theirs = lax.optimization_barrier((cross_q[0], cross_theirs))
    cross_theirs = lax.ppermute(cross_theirs, "seq", TO_CORE)
    cross_mine = cross(own_cross_q, False)

    def join(a, b):
        return call(join_kernel, "join", [], [a, b], jax.ShapeDtypeStruct((ROWS, H * DH), BF16), [], 1)

    self_out = join(mine, self_theirs)
    cross_out = join(cross_mine, cross_theirs)
    return self_out[None], cross_out[None]


def solution(mesh):
    rows = P("grp", "seq", None)
    return jax.shard_map(
        per_device,
        mesh=mesh,
        in_specs=(rows, rows, rows, rows, rows, rows, P(), P()),
        out_specs=(rows, rows),
        check_vma=False,
    )
```

time: 301 us -> 294 us (0.977)
  the two profiles are of different devices: /device:TPU:385 before, /device:TPU:410 now
where the time goes in v2:
time: 294 us; the launch traced here: 293 us
  Pallas kernels  213 us (72%)
  starting transfers between devices  31.4 us (11%)
  waiting for transfers between devices  29.2 us (10%)
  between operations  14.2 us (5%)
  local copies, waits for them, and re-layouts  4.24 us (1%)
    pallas_call x5, Pallas kernels, call(): pl.pallas_call(kernel, out_shape=outs, in_specs=[pl.BlockSpec(memory_spac...  213 us
    all_gather x1, waiting for transfers between devices, per_device(): lax.all_gather(jnp.stack([own, across]), 'seq', axis_index_groups=Z_GROUPS)  14.3 us
    all_to_all x1, starting transfers between devices, per_device(): lax.all_to_all(jnp.broadcast_to(piece, (YH * Y * Z, *piece.shape)), ('grp...  11 us
    all_to_all x1, waiting for transfers between devices, per_device(): lax.all_to_all(jnp.broadcast_to(piece, (YH * Y * Z, *piece.shape)), ('grp...  10.1 us
    ppermute x3, starting transfers between devices, per_device(): lax.ppermute(column, 'grp', to_x(-shift))  9.87 us
  transfers between devices with their start and end apart: 10, of which 3 were waited for; matrix products, arithmetic and copies ran while one was open for 1% of the time, Pallas kernels for 72%

profile of v2, /device:TPU:410, one launch (start us, length us, event | category | flops | bytes accessed | tf_op | source)
XLA Modules:
  0.0 293.5 jit_solution(12016939816385392195)
XLA Ops:
  7.2 0.0 all-gather.3.cloned.1.call-start
  7.2 0.8 constant_dynamic-update-slice_fusion.1
  8.1 0.9 constant_dynamic-update-slice_fusion
  8.9 2.4 collective-permute-start.2
  11.3 4.8 %collective-permute-done.2 = bf16[2,256,128]{2,1,0:T(8,128)(2,1)S(1)} collective-permute-done((bf16[2,256,128]{2,1,0:T(8,128)(2,1)S(1)}, bf16[2,256,128]{2,1,0:T(8,128)(2,1)S(1)}, u32[]{:S(2)}, u32[]{:S(2)}) %collective-permute-start.2) | collective-permute-done | bytes 131104 | tf_op jit(solution)/shard_map/ppermute | solution.py:234
  16.0 0.7 pad_maximum_fusion
  16.8 0.0 all-gather.3.cloned.1.call-update
  16.8 0.7 pad_maximum_fusion.1
  17.5 0.9 broadcast_in_dim.10
  18.4 11.0 %all-to-all-start = ((bf16[64,2,16,128]{3,2,1,0:T(8,128)(2,1)}), bf16[64,2,16,128]{3,2,1,0:T(8,128)(2,1)S(1)}, u32[]{:S(2)}, u32[]{:S(2)}) async-start(bf16[64,2,16,128]{3,2,1,0:T(8,128)(2,1)} %broadcast_in_dim.10), calls=%async_computation | async-start | bytes 1048576 | tf_op jit(solution)/shard_map/all_to_all | solution.py:240
  29.4 1.9 collective-permute-start.1
  31.3 2.4 collective-permute-start
  33.7 0.1 copy.13.mask
  33.8 0.1 pad_add_fusion.place
  33.9 10.1 %all-to-all-done = bf16[64,2,16,128]{3,2,1,0:T(8,128)(2,1)S(1)} async-done(((bf16[64,2,16,128]{3,2,1,0:T(8,128)(2,1)}), bf16[64,2,16,128]{3,2,1,0:T(8,128)(2,1)S(1)}, u32[]{:S(2)}, u32[]{:S(2)}) %all-to-all-start) | async-done | bytes 524320 | tf_op jit(solution)/shard_map/all_to_all | solution.py:240
  44.0 3.4 %collective-permute-start.4 = (bf16[4,16,2,16,128]{4,3,2,1,0:T(8,128)(2,1)S(1)}, bf16[4,16,2,16,128]{4,3,2,1,0:T(8,128)(2,1)S(1)}, u32[]{:S(2)}, u32[]{:S(2)}) collective-permute-start(bf16[4,16,2,16,128]{4,3,2,1,0:T(8,128)(2,1)S(1)} %bitcast.10), channel_id=1, source_target_pairs={{0,1},{1,2},{2,3},{3,0},{4,5},{5,6},{6,7},{7,4},{8,9},{9,10},{10,1... | collective-permute-start | bytes 1572872 | tf_op jit(solution)/shard_map/ppermute | solution.py:244
  47.4 2.4 collective-permute-start.5
  49.8 4.0 %collective-permute-start.6 = (bf16[4,16,2,16,128]{4,3,2,1,0:T(8,128)(2,1)S(1)}, bf16[4,16,2,16,128]{4,3,2,1,0:T(8,128)(2,1)}, u32[]{:S(2)}, u32[]{:S(2)}) collective-permute-start(bf16[4,16,2,16,128]{4,3,2,1,0:T(8,128)(2,1)S(1)} %bitcast.12), channel_id=1, source_target_pairs={{0,2},{1,3},{2,0},{3,1},{4,6},{5,7},{6,4},{7,5},{8,10},{9,11},{10,... | collective-permute-start | bytes 1572872 | tf_op jit(solution)/shard_map/ppermute | solution.py:244
  53.9 0.0 collective-permute-done.1.partner_ref
  53.9 14.3 %all-gather.3.cloned.1.call-done = bf16[16,2,256,128]{3,2,1,0:T(8,128)(2,1)} async-done(((bf16[2,2,256,128]{3,2,1,0:T(8,128)(2,1)}), bf16[16,2,256,128]{3,2,1,0:T(8,128)(2,1)}) %all-gather.3.cloned.1.call-update) | async-done | bytes 2097168 | tf_op jit(solution)/shard_map/all_gather | solution.py:237
  68.2 1.6 copy-done
  69.8 161.9 %own.1 = (f32[8,144,256]{2,1,0:T(8,128)S(1)}, f32[8,144,256]{2,1,0:T(8,128)S(1)}) custom-call(s32[2]{0:T(128)S(1)} %pad_add_fusion.place, s32[32]{0:T(128)S(1)} %copy-done.3, bf16[256,1024]{1,0:T(8,128)(2,1)S(1)} %bitcast.17, bf16[256,1024]{1,0:T(8,128)(2,1)S(1)} %collective-permute-done.1.partner_ref, bf16[8,2,2,256,128]{4,3,2,1,0:T(8,128)(2,1)S(1)} %bitcast.15), custom_call_target="tpu_custom_call" | custom-call | flops 8589934592 | bytes 4194304 | tf_op jit(solution)/shard_map/own/pallas_call | solution.py:215
  231.7 0.0 collective-permute-done.q_ref
  231.7 1.9 collective-permute-start.3
  233.7 0.0 collective-permute-done.4.refs_1_
  233.7 0.0 collective-permute-done.5.refs_2_
  233.7 21.9 %cross.2 = f32[8,144,256]{2,1,0:T(8,128)S(1)} custom-call(s32[2]{0:T(128)S(1)} %pad_add_fusion.place, s32[32]{0:T(128)S(1)} %copy-done.3, s32[32,16]{1,0:T(8,128)S(1)} %copy.13.mask, bf16[256,1024]{1,0:T(8,128)(2,1)S(1)} %collective-permute-done.q_ref, bf16[4,16,2,16,128]{4,3,2,1,0:T(8,128)(2,1)S(1)} %bitcast.13, ...), custom_call_target="tpu_custom_call" | custom-call | flops 2684354560 | bytes 4194304 | tf_op jit(solution)/shard_map/cross/pallas_call | solution.py:215
  255.6 1.9 collective-permute-start.7
  257.5 26.9 %cross.3.mine = f32[8,144,256]{2,1,0:T(8,128)S(1)} custom-call(s32[2]{0:T(128)S(1)} %pad_add_fusion.place, s32[32]{0:T(128)S(1)} %copy-done.3, s32[32,16]{1,0:T(8,128)S(1)} %copy.13.mask, bf16[256,1024]{1,0:T(8,128)(2,1)S(1)} %bitcast.19, bf16[4,16,2,16,128]{4,3,2,1,0:T(8,128)(2,1)S(1)} %bitcast.14, ...), custom_call_target="tpu_custom_call" | custom-call | flops 2684354560 | bytes 4194304 | tf_op jit(solution)/shard_map/cross/pallas_call | solution.py:215
  284.5 0.0 collective-permute-done.3.theirs
  284.5 1.1 join.2
  285.6 1.1 join.3
  (11 shorter events, 0.0 us)
Async XLA Ops:
  7.2 61.1 %all-gather.3.cloned.1.call-start = ((), (), s32[]{:S(2)}) async-start(), calls=%async_computation.1 | async-start | bytes 2359296 | tf_op jit(solution)/shard_map/all_gather | solution.py:237
  8.9 7.1 %collective-permute-start.2 = (bf16[2,256,128]{2,1,0:T(8,128)(2,1)S(1)}, bf16[2,256,128]{2,1,0:T(8,128)(2,1)S(1)}, u32[]{:S(2)}, u32[]{:S(2)}) collective-permute-start(bf16[2,256,128]{2,1,0:T(8,128)(2,1)S(1)} %constant_dynamic-update-slice_fusion), channel_id=1, source_target_pairs={{0,256},{16,272},{32,288},{48,304},{64,320},{80,336},{96,352},{112... | collective-permute-start | bytes 393224 | tf_op jit(solution)/shard_map/ppermute | solution.py:234
  16.0 13.3 %copy-start.1 = (bf16[1,256,1024]{2,1,0:T(8,128)(2,1)S(1)}, bf16[1,256,1024]{2,1,0:T(8,128)(2,1)}, u32[]{:S(2)}) copy-start(bf16[1,256,1024]{2,1,0:T(8,128)(2,1)} %param.8) | copy-start | bytes 1572868
  16.0 15.3 %copy-start.2 = (bf16[1,256,1024]{2,1,0:T(8,128)(2,1)S(1)}, bf16[1,256,1024]{2,1,0:T(8,128)(2,1)}, u32[]{:S(2)}) copy-start(bf16[1,256,1024]{2,1,0:T(8,128)(2,1)} %param.9) | copy-start | bytes 1572868
  16.0 17.7 %copy-start.4 = (s32[32,16]{0,1:T(8,128)S(1)}, s32[32,16]{0,1:T(8,128)}, u32[]{:S(2)}) copy-start(s32[32,16]{0,1:T(8,128)} %param.15) | copy-start | bytes 6148
  16.0 52.2 %copy-start.3 = (s32[32]{0:T(128)S(1)}, s32[32]{0:T(128)}, u32[]{:S(2)}) copy-start(s32[32]{0:T(128)} %block_pos.5) | copy-start | bytes 388
  18.4 25.6 %all-to-all-start = ((bf16[64,2,16,128]{3,2,1,0:T(8,128)(2,1)}), bf16[64,2,16,128]{3,2,1,0:T(8,128)(2,1)S(1)}, u32[]{:S(2)}, u32[]{:S(2)}) async-start(bf16[64,2,16,128]{3,2,1,0:T(8,128)(2,1)} %broadcast_in_dim.10), calls=%async_computation | async-start | bytes 1048576 | tf_op jit(solution)/shard_map/all_to_all | solution.py:240
  29.4 24.5 %collective-permute-start.1 = (bf16[256,1024]{1,0:T(8,128)(2,1)S(1)}, bf16[256,1024]{1,0:T(8,128)(2,1)S(1)}, u32[]{:S(2)}, u32[]{:S(2)}) collective-permute-start(bf16[256,1024]{1,0:T(8,128)(2,1)S(1)} %bitcast.16), channel_id=1, source_target_pairs={{0,16},{16,0},{32,48},{48,32},{64,80},{80,64},{96,112},{112,96},{1... | collective-permute-start | bytes 1572872 | tf_op jit(solution)/shard_map/ppermute | solution.py:235
  31.3 200.4 %collective-permute-start = (bf16[256,1024]{1,0:T(8,128)(2,1)S(1)}, bf16[256,1024]{1,0:T(8,128)(2,1)S(1)}, u32[]{:S(2)}, u32[]{:S(2)}) collective-permute-start(bf16[256,1024]{1,0:T(8,128)(2,1)S(1)} %bitcast.18), channel_id=1, source_target_pairs={{0,16},{16,0},{32,48},{48,32},{64,80},{80,64},{96,112},{112,96},{1... | collective-permute-start | bytes 1572872 | tf_op jit(solution)/shard_map/ppermute | solution.py:236
  44.0 189.7 %collective-permute-start.4 = (bf16[4,16,2,16,128]{4,3,2,1,0:T(8,128)(2,1)S(1)}, bf16[4,16,2,16,128]{4,3,2,1,0:T(8,128)(2,1)S(1)}, u32[]{:S(2)}, u32[]{:S(2)}) collective-permute-start(bf16[4,16,2,16,128]{4,3,2,1,0:T(8,128)(2,1)S(1)} %bitcast.10), channel_id=1, source_target_pairs={{0,1},{1,2},{2,3},{3,0},{4,5},{5,6},{6,7},{7,4},{8,9},{9,10},{10,1... | collective-permute-start | bytes 1572872 | tf_op jit(solution)/shard_map/ppermute | solution.py:244
  47.4 186.3 %collective-permute-start.5 = (bf16[4,16,2,16,128]{4,3,2,1,0:T(8,128)(2,1)S(1)}, bf16[4,16,2,16,128]{4,3,2,1,0:T(8,128)(2,1)}, u32[]{:S(2)}, u32[]{:S(2)}) collective-permute-start(bf16[4,16,2,16,128]{4,3,2,1,0:T(8,128)(2,1)S(1)} %bitcast.11), channel_id=1, source_target_pairs={{0,3},{1,0},{2,1},{3,2},{4,7},{5,4},{6,5},{7,6},{8,11},{9,8},{10,9... | collective-permute-start | bytes 1572872 | tf_op jit(solution)/shard_map/ppermute | solution.py:244
  49.8 183.8 %collective-permute-start.6 = (bf16[4,16,2,16,128]{4,3,2,1,0:T(8,128)(2,1)S(1)}, bf16[4,16,2,16,128]{4,3,2,1,0:T(8,128)(2,1)}, u32[]{:S(2)}, u32[]{:S(2)}) collective-permute-start(bf16[4,16,2,16,128]{4,3,2,1,0:T(8,128)(2,1)S(1)} %bitcast.12), channel_id=1, source_target_pairs={{0,2},{1,3},{2,0},{3,1},{4,6},{5,7},{6,4},{7,5},{8,10},{9,11},{10,... | collective-permute-start | bytes 1572872 | tf_op jit(solution)/shard_map/ppermute | solution.py:244
  68.2 1.6 copy-start
  231.7 52.8 %collective-permute-start.3 = (f32[8,144,256]{2,1,0:T(8,128)S(1)}, f32[8,144,256]{2,1,0:T(8,128)S(1)}, u32[]{:S(2)}, u32[]{:S(2)}) collective-permute-start(f32[8,144,256]{2,1,0:T(8,128)S(1)} %get-tuple-element.10), channel_id=1, source_target_pairs={{0,16},{16,0},{32,48},{48,32},{64,80},{80,64},{96,112},{112,96},{1... | collective-permute-start | bytes 3538952 | tf_op jit(solution)/shard_map/ppermute | solution.py:250
  255.6 30.0 %collective-permute-start.7 = (f32[8,144,256]{2,1,0:T(8,128)S(1)}, f32[8,144,256]{2,1,0:T(8,128)S(1)}, u32[]{:S(2)}, u32[]{:S(2)}) collective-permute-start(f32[8,144,256]{2,1,0:T(8,128)S(1)} %cross.2), channel_id=1, source_target_pairs={{0,16},{16,0},{32,48},{48,32},{64,80},{80,64},{96,112},{112,96},{1... | collective-permute-start | bytes 3538952 | tf_op jit(solution)/shard_map/ppermute | solution.py:261
Sparse Core Ops, SparseCore 0:
  16.9 51.2 all-gather.2
